TPU v7x, 128 devices: a whole 4x4x4 slice. The times are simulated.
128 devices in a mesh: dom: 128 (over x, z, y, core).
Axes of the slice: x: 4, y: 4, z: 4, core: 2. Of those that a mesh axis runs over, the one named last changes fastest.
Arguments:
- states: bfloat16 [262144, 768], P('dom'), may hold values from -6 to 6
- pre_act: bfloat16 [262144, 768], P('dom'), may hold values from -6 to 6
- features: bfloat16 [262144, 256], P('dom'), may hold values from -6 to 6
- cotangent: bfloat16 [262144, 256], P('dom'), may hold values from -6 to 6
- halo_states: bfloat16 [73728, 768], P('dom'), may hold values from -6 to 6
- halo_cot: bfloat16 [73728, 768], P('dom'), may hold values from -2 to 2
- coupling: bfloat16 [262144, 576], P('dom'), may hold values from -0.25 to 0.25
- tile_blocks: bfloat16 [8192, 128, 128], P('dom'), may hold values from -0.25 to 0.25
- tile_rows: int32 [8192], P('dom'), may hold values from 0 to 15
- tile_cols: int32 [8192], P('dom'), may hold values from 0 to 15
- tile_counts: int32 [128], P('dom'), may hold values from 16 to 64, as said below
- send_rows: int32 [1152, 64], P('dom'), may hold values from 0 to 2047
- send_counts: int32 [1152], P('dom'), may hold values from 22 to 64, as said below
- recv_counts: int32 [1152], P('dom'), may hold values from 22 to 64, as said below
- w_state: bfloat16 [3, 256, 256], replicated, may hold values from -0.375 to 0.375
- w_input: bfloat16 [3, 256, 256], replicated, may hold values from -0.375 to 0.375
Outputs:
- state_grad: bfloat16 [262144, 768], P('dom')
- feature_grad: bfloat16 [262144, 256], P('dom')
- weight_grad: float32 [3, 256, 256], replicated
- input_grad: float32 [3, 256, 256], replicated
- sent_cot: bfloat16 [73728, 768], P('dom')
Inputs may be any that keep to these rules, and one draw needn't show every extreme that they name: `send_counts`: partition p sends slot j to partition (p + offset_j) mod 128; some slot of some partition holds exactly 64 rows in every draw. recv_counts[q * 9 + j] equals send_counts[p * 9 + j] for p = (q - offset_j) mod 128. `tile_counts`: some partition has all 64 slots live in every draw.
All inputs are finite; a program needn't handle non-finite values.
Results may differ from a plain program's by a relative error of at most 0.0055.
Values may be sent and summed in bfloat16 or wider, within the bound.
A program may use at most 192 MiB of HBM per device.

v0:
```python
from types import SimpleNamespace

import jax
import jax.numpy as jnp
from jax import lax
from jax.experimental import pallas as pl
from jax.experimental.pallas import tpu as pltpu
from jax.sharding import PartitionSpec as P

MESH = pl.DeviceIdType.MESH
F32 = jnp.float32
BF16 = jnp.bfloat16

OFFSETS = (1, 2, 3, 4, -1, -2, -3, -4, 64)
SLOTS = 9
CAP = 64
NT = (((1,), (1,)), ((), ()))
TN = (((0,), (0,)), ((), ()))


def dot(a, b):
    return jnp.dot(a, b, preferred_element_type=F32)


def dot_nt(a, b):
    return lax.dot_general(a, b, NT, preferred_element_type=F32)


def dot_tn(a, b):
    return lax.dot_general(a, b, TN, preferred_element_type=F32)


def order_tiles(r):
    r.load_tile_rows.wait()
    r.load_tile_cols.wait()
    count = r.tile_counts[0]
    sub = lax.broadcasted_iota(jnp.int32, (8, 128), 0)
    tile = lax.broadcasted_iota(jnp.int32, (64, 128), 0)
    lane = lax.broadcasted_iota(jnp.int32, (64, 128), 1)
    lane1 = lax.broadcasted_iota(jnp.int32, (1, 128), 1)
    zero = jnp.zeros((64, 128), jnp.int32)
    keys, rows = [], []
    for t in range(64):
        keys.append(jnp.where(t < count, r.s_tile_cols[t], 16))
        rows.append(r.s_tile_rows[t])

    def column(values):
        parts = []
        for b in range(8):
            part = jnp.zeros((8, 128), jnp.int32)
            for i in range(8):
                part = jnp.where(sub == i, values[8 * b + i], part)
            parts.append(part)
        return jnp.concatenate(parts, axis=0)

    key, row = column(keys), column(rows)
    place = zero
    for s in range(64):
        place += jnp.where((key == keys[s]) & (tile > s), 1, 0)
    base = zero
    upto = jnp.zeros((1, 128), jnp.int32)
    inside = jnp.zeros((1, 128), jnp.int32)
    for c in range(16):
        here = jnp.sum(jnp.where(key == c, 1, 0), axis=0, keepdims=True)
        pairs = (here + 1) >> 1
        base += jnp.where(key > c, pairs, 0)
        upto += jnp.where(lane1 >= c, pairs, 0)
        inside += jnp.where(lane1 == c, here, 0)
    at = jnp.where(key < 16, base + (place >> 1), 1000)
    first = (at == lane) & ((place & 1) == 0)
    second = (at == lane) & ((place & 1) == 1)

    def total(mask, value):
        return jnp.sum(jnp.where(mask, value, 0), axis=0, keepdims=True)

    meta = (total(first, tile - 64) + 64, total(second, tile - 64) + 64, total(first, row), total(second, row), total(first & (place > 0), 1), upto, inside)
    for i, value in enumerate(meta):
        r.v_meta[i : i + 1, :] = value
    r.v_meta[7:8, :] = jnp.zeros((1, 128), jnp.int32)
    pltpu.make_async_copy(r.v_meta, r.meta, r.meta_sem).start()


def make_pre_grad(r):
    for i in range(4):
        r.load_acts[i].wait()
        r.load_cots[i].wait()

        @pl.loop(0, 4)
        def _(b):
            rows = pl.ds(pl.multiple_of(512 * i + 128 * b, 128), 128)
            third = (r.ct[rows, :].astype(F32) * (1.0 / 3.0)).astype(BF16)
            for k in range(3):
                cols = slice(256 * k, 256 * k + 256)
                act = r.pg[rows, cols]
                r.pg[rows, cols] = jnp.where(act > 0, third, jnp.zeros_like(third))


def make_one_hot(r):
    r.load_send_rows.wait()
    index = r.v_send_rows[...].T
    slot = lax.broadcasted_iota(jnp.int32, (CAP, 1), 0)
    node = lax.broadcasted_iota(jnp.int32, (CAP, 2048), 1)
    for j in range(SLOTS):
        mine = jnp.where(slot < r.send_counts[j], index[:, j : j + 1], -1)
        r.oh[CAP * j : CAP * j + CAP, :] = jnp.where(node == mine, 1.0, 0.0).astype(BF16)


def make_outgoing(r, k):
    cols = slice(256 * k, 256 * k + 256)
    r.outgoing[:, cols] = dot(r.oh[...], r.pg[:, cols]).astype(BF16)


def make_feature_grad(r):
    @pl.loop(0, 2)
    def _(b):
        rows = pl.ds(pl.multiple_of(1024 * b, 1024), 1024)
        total = dot_nt(r.pg[rows, 0:256], r.w_input[0])
        for k in (1, 2):
            total += dot_nt(r.pg[rows, 256 * k : 256 * k + 256], r.w_input[k])
        r.feature_grad[rows, :] = total.astype(BF16)


def make_v(r):
    r.load_features.wait()
    for b in range(2):
        rows = pl.ds(1024 * b, 1024)
        left = r.v_features[rows, :].T
        for k in range(3):
            part = dot(left, r.pg[rows, 256 * k : 256 * k + 256])
            r.gacc[0, k] = part if b == 0 else r.gacc[0, k] + part


def mask_halo(r, ref):
    slot = lax.broadcasted_iota(jnp.int32, (CAP, 768), 0)
    for j in range(SLOTS):
        rows = slice(CAP * j, CAP * j + CAP)
        ref[rows, :] = jnp.where(slot < r.recv_counts[j], ref[rows, :].astype(F32), 0.0).astype(BF16)


def flip_tiles(r):
    r.v_tile_blocks[64] = jnp.zeros((128, 128), BF16)
    r.load_tile_blocks.wait()

    @pl.loop(0, 64, unroll=16)
    def _(t):
        r.v_tile_blocks[t] = r.v_tile_blocks[t].T


def make_q(r, k):
    cols = slice(256 * k, 256 * k + 256)
    meta, tiles = r.meta, r.v_tile_blocks

    @pl.loop(0, 40, unroll=20)
    def _(t):
        up = pl.ds(pl.multiple_of(meta[2, t] * 128, 128), 128)
        low = pl.ds(pl.multiple_of(meta[3, t] * 128, 128), 128)
        left = jnp.concatenate([tiles[meta[0, t]], tiles[meta[1, t]]], axis=1)
        right = jnp.concatenate([r.pg[up, cols], r.pg[low, cols]], axis=0)
        r.stage[t + 1] = dot(left, right) + jnp.where(meta[4, t] > 0, r.stage[t], 0.0)

    @pl.loop(0, 16, unroll=8)
    def _(c):
        value = jnp.where(meta[6, c] > 0, r.stage[meta[5, c]], 0.0)
        r.qb[pl.ds(pl.multiple_of(c * 128, 128), 128), cols] = value.astype(BF16)


def make_w(r, k):
    cols = slice(256 * k, 256 * k + 256)
    meet = dot(r.coupling[...], r.pg[:, cols]).astype(BF16)
    r.gacc[1, k] = dot_tn(r.v_halo_states[:, cols], meet)
    for b in range(2):
        rows = pl.ds(1024 * b, 1024)
        r.gacc[1, k] += dot_tn(r.states[rows, cols], r.qb[rows, cols])


def make_e(r):
    r.load_halo_cot.wait()
    mask_halo(r, r.v_halo_cot)
    for k in range(3):
        cols = slice(256 * k, 256 * k + 256)
        r.ee[:, cols] = dot_nt(r.v_halo_cot[:, cols], r.w_state[k]).astype(BF16)


def make_state_grad(r, half):
    @pl.loop(0, 2)
    def _(b):
        rows = pl.ds(pl.multiple_of(1024 * half + 512 * b, 512), 512)
        left = r.coupling[:, rows].T
        for k in range(3):
            cols = slice(256 * k, 256 * k + 256)
            total = dot(left, r.ee[:, cols]) + dot_nt(r.qb[rows, cols], r.w_state[k])
            r.state_grad[rows, cols] = total.astype(BF16)


class Place:
    def __init__(self):
        self.me = lax.axis_index("dom")
        self.x = lax.div(self.me, 32)
        self.z = lax.rem(lax.div(self.me, 8), 4)
        self.y = lax.rem(lax.div(self.me, 2), 4)
        self.core = lax.rem(self.me, 2)
        self.own = self.x * 4 + self.z
        self.xs = [lax.rem(self.x + j, 4) for j in range(4)]
        self.zs = [lax.rem(self.z + j, 4) for j in range(4)]
        self.sibling = self.me + 1 - 2 * self.core
        low = self.y * 2 + self.core
        self.plane = []
        for n in FAR_FIRST:
            to = self.xs[n // 4] * 4 + self.zs[n % 4]
            self.plane.append((n, to, to * 8 + low))
        base = self.me - self.y * 2
        self.line = [base + 2 * lax.rem(self.y + j, 4) for j in (1, 2, 3)]
        self.halo = [lax.rem(self.me + 128 + offset, 128) for offset in OFFSETS]


FAR_FIRST = (10, 6, 14, 9, 11, 5, 7, 13, 15, 2, 8, 1, 3, 4, 12)


def remote(src, dst, send, recv, device):
    return pltpu.make_async_remote_copy(src_ref=src, dst_ref=dst, send_sem=send, recv_sem=recv, device_id=(device,), device_id_type=MESH)


def greet(at):
    barrier = pltpu.get_barrier_semaphore()
    for device in [at.sibling] + [device for _, _, device in at.plane] + at.line + at.halo:
        pl.semaphore_signal(barrier, inc=1, device_id=(device,), device_id_type=MESH)


def await_greetings():
    pl.semaphore_wait(pltpu.get_barrier_semaphore(), 1 + 15 + 3 + SLOTS)


def halo_copy(r, at, j):
    rows = pl.ds(CAP * j, CAP)
    return remote(r.outgoing.at[rows], r.sent_cot.at[rows], r.halo_send.at[j], r.halo_recv.at[j], at.halo[j])


def core_copy(at, g):
    return remote(g.half, g.core, g.a_send, g.a_recv, at.sibling)


def scatter_all(at, g):
    return remote(g.r1, g.r1, g.b_send, g.b_recv, at.sibling)


def line_copy(at, g, j):
    mine = g.r2.at[at.y]
    return remote(mine, mine, g.c_send.at[j], g.c_recv.at[j], at.line[j])


def gather_all(at, g):
    every = g.fin.at[0, pl.ds(0, 15)]
    return remote(every, every, g.d_send, g.d_recv, at.sibling)


def sibling_copy(at, g):
    mine = g.fin.at[at.core]
    return remote(mine, mine, g.e_send, g.e_recv, at.sibling)


def reduce_core(r, at, g):
    theirs = pl.ds(pl.multiple_of((1 - at.core) * 128, 128), 128)
    for i in range(g.count):
        g.half[i] = r.gacc[g.p, g.k + i, :, theirs].astype(BF16)
    core_copy(at, g).start()


def reduce_plane(r, at, g):
    ours = pl.ds(pl.multiple_of(at.core * 128, 128), 128)
    core_copy(at, g).wait_recv()
    for i in range(g.count):
        total = r.gacc[g.p, g.k + i, :, ours] + g.core[i].astype(F32)
        g.sum[i] = total
        g.send[:, i] = total.reshape(16, 16, 128).astype(BF16)
    for n, to, device in at.plane:
        remote(g.send.at[to], g.r1.at[n - 1], g.b_send, g.b_recv, device).start()


def reduce_line(r, at, g):
    rows = pl.ds(pl.multiple_of(at.own * 16, 16), 16)
    total = g.sum[:, rows, :]
    scatter_all(at, g).wait_recv()
    for n in range(15):
        total += g.r1[n].astype(F32)
    g.r2[at.y] = total
    for j in range(3):
        line_copy(at, g, j).start()


def gather_plane(r, at, g):
    for j in range(3):
        line_copy(at, g, j).wait_recv()
    total = (g.r2[0] + g.r2[1]) + (g.r2[2] + g.r2[3])
    g.fin[at.core, at.own] = total.astype(BF16)
    mine = g.fin.at[at.core, at.own]
    for _, _, device in at.plane:
        remote(mine, mine, g.d_send, g.d_recv, device).start()


def gather_core(r, at, g):
    gather_all(at, g).wait_recv()
    sibling_copy(at, g).start()


def gather_end(r, at, g):
    out = r.weight_grad if g.p else r.input_grad
    sibling_copy(at, g).wait_recv()
    for i in range(g.count):
        for c in range(2):
            block = g.fin[c, :, i].astype(F32).reshape(256, 128)
            out[g.k + i, :, 128 * c : 128 * c + 128] = block * (1.0 / 512.0)


def drain(r, at):
    for g in r.groups:
        core_copy(at, g).wait_send()
        scatter_all(at, g).wait_send()
        for j in range(3):
            line_copy(at, g, j).wait_send()
        gather_all(at, g).wait_send()
        sibling_copy(at, g).wait_send()
    for j in range(SLOTS):
        halo_copy(r, at, j).wait()


GROUPS = ((0, 0, 3), (1, 0, 1), (1, 1, 1), (1, 2, 1))
DMA = pltpu.SemaphoreType.DMA


def group_scratch(count):
    one = DMA(())
    return dict(
        half=pltpu.VMEM((count, 256, 128), BF16),
        core=pltpu.VMEM((count, 256, 128), BF16),
        sum=pltpu.VMEM((count, 256, 128), F32),
        send=pltpu.VMEM((16, count, 16, 128), BF16),
        r1=pltpu.VMEM((15, count, 16, 128), BF16),
        r2=pltpu.VMEM((4, count, 16, 128), F32),
        fin=pltpu.VMEM((2, 16, count, 16, 128), BF16),
        a_send=one, a_recv=one, b_send=one, b_recv=one, c_send=DMA((3,)), c_recv=DMA((3,)),
        d_send=one, d_recv=one, e_send=one, e_recv=one,
    )


TILES_SCRATCH = dict(
    ct=pltpu.VMEM((2048, 256), BF16),
    v_tile_blocks=pltpu.VMEM((65, 128, 128), BF16),
    stage=pltpu.VMEM((41, 128, 256), F32),
    meta=pltpu.SMEM((8, 128), jnp.int32),
    v_meta=pltpu.VMEM((8, 128), jnp.int32),
    s_tile_rows=pltpu.SMEM((64,), jnp.int32),
    s_tile_cols=pltpu.SMEM((64,), jnp.int32),
    in_sem=DMA((11,)),
    meta_sem=DMA(()),
)


def tiles_kernel(tile_counts, tile_rows, tile_cols, pre_act, cotangent, tile_blocks, pg, qb, *scratch):
    r = SimpleNamespace(**dict(zip(TILES_SCRATCH, scratch, strict=True)), tile_counts=tile_counts, pg=pg, qb=qb)

    def load(i, src, dst):
        copy = pltpu.make_async_copy(src, dst, r.in_sem.at[i])
        copy.start()
        return copy

    r.load_tile_rows = load(0, tile_rows, r.s_tile_rows)
    r.load_tile_cols = load(1, tile_cols, r.s_tile_cols)
    parts = [pl.ds(512 * i, 512) for i in range(4)]
    r.load_cots, r.load_acts = [], []
    for i, rows in enumerate(parts):
        r.load_cots.append(load(2 + i, cotangent.at[rows], r.ct.at[rows]))
        r.load_acts.append(load(6 + i, pre_act.at[rows], pg.at[rows]))
    r.load_tile_blocks = load(10, tile_blocks, r.v_tile_blocks.at[pl.ds(0, 64)])
    order_tiles(r)
    r.stage[0] = jnp.zeros((128, 256), F32)
    make_pre_grad(r)
    flip_tiles(r)
    pltpu.make_async_copy(r.v_meta, r.meta, r.meta_sem).wait()
    for k in range(3):
        make_q(r, k)


REST_SCRATCH = dict(
    v_send_rows=pltpu.VMEM((9, 64), jnp.int32),
    v_features=pltpu.VMEM((2048, 256), BF16),
    v_halo_states=pltpu.VMEM((576, 768), BF16),
    v_halo_cot=pltpu.VMEM((576, 768), BF16),
    oh=pltpu.VMEM((576, 2048), BF16),
    ee=pltpu.VMEM((576, 768), BF16),
    outgoing=pltpu.VMEM((576, 768), BF16),
    gacc=pltpu.VMEM((2, 3, 256, 256), F32),
    in_sem=DMA((4,)),
    halo_send=DMA((9,)),
    halo_recv=DMA((9,)),
)


def rest_refs(send_counts, recv_counts, pg, qb, states, features, halo_states, halo_cot, coupling, send_rows, w_state, w_input, state_grad, feature_grad, weight_grad, input_grad, sent_cot, *scratch):
    scratch = list(scratch)
    own = dict(zip(REST_SCRATCH, scratch))
    del scratch[: len(own)]
    r = SimpleNamespace(**own, send_counts=send_counts, recv_counts=recv_counts, pg=pg, qb=qb, states=states, coupling=coupling, w_state=w_state, w_input=w_input)
    r.state_grad, r.feature_grad, r.weight_grad, r.input_grad, r.sent_cot = state_grad, feature_grad, weight_grad, input_grad, sent_cot
    r.groups = []
    for p, k, count in GROUPS:
        kinds = group_scratch(count)
        r.groups.append(SimpleNamespace(**dict(zip(kinds, scratch)), p=p, k=k, count=count))
        del scratch[: len(kinds)]

    def load(i, src, dst):
        copy = pltpu.make_async_copy(src, dst, r.in_sem.at[i])
        copy.start()
        return copy

    r.load_halo_states = load(0, halo_states, r.v_halo_states)
    r.load_features = load(1, features, r.v_features)
    r.load_send_rows = load(2, send_rows, r.v_send_rows)
    r.load_halo_cot = load(3, halo_cot, r.v_halo_cot)
    return r


def rest_kernel(*refs):
    r = rest_refs(*refs)
    v, w0, w1, w2 = r.groups
    at = Place()
    greet(at)

    def halo(*slots):
        for j in slots:
            halo_copy(r, at, j).start()

    r.load_halo_states.wait()
    mask_halo(r, r.v_halo_states)
    make_w(r, 0)
    await_greetings()
    reduce_core(r, at, w0)
    make_w(r, 1)
    reduce_core(r, at, w1)
    reduce_plane(r, at, w0)
    make_w(r, 2)
    reduce_core(r, at, w2)
    reduce_plane(r, at, w1)
    make_v(r)
    reduce_core(r, at, v)
    reduce_plane(r, at, w2)
    make_one_hot(r)
    make_outgoing(r, 0)
    reduce_line(r, at, w0)
    reduce_plane(r, at, v)
    make_outgoing(r, 1)
    make_outgoing(r, 2)
    halo(2, 6)
    reduce_line(r, at, w1)
    make_e(r)
    reduce_line(r, at, w2)
    gather_plane(r, at, w0)
    halo(3, 7)
    make_feature_grad(r)
    gather_plane(r, at, w1)
    reduce_line(r, at, v)
    make_state_grad(r, 0)
    gather_plane(r, at, w2)
    halo(1, 5)
    gather_core(r, at, w0)
    make_state_grad(r, 1)
    gather_plane(r, at, v)
    halo(0, 4, 8)
    gather_end(r, at, w0)
    gather_core(r, at, w1)
    gather_core(r, at, w2)
    gather_end(r, at, w1)
    gather_end(r, at, w2)
    gather_core(r, at, v)
    gather_end(r, at, v)
    drain(r, at)


def move_kernel(*refs):
    sem = refs[-1]
    copies = [pltpu.make_async_copy(refs[i], refs[5 + i], sem.at[i]) for i in range(5)]
    for copy in copies:
        copy.start()
    for copy in copies:
        copy.wait()


def shards(states, pre_act, features, cotangent, halo_states, halo_cot, coupling, tile_blocks, tile_rows, tile_cols, tile_counts, send_rows, send_counts, recv_counts, w_state, w_input):
    far = pl.BlockSpec(memory_space=pl.ANY)
    smem = pl.BlockSpec(memory_space=pltpu.SMEM)
    vmem = pl.BlockSpec(memory_space=pltpu.VMEM)
    wide = jax.ShapeDtypeStruct((2048, 768), BF16)
    results = (
        wide,
        jax.ShapeDtypeStruct((2048, 256), BF16),
        jax.ShapeDtypeStruct((3, 256, 256), F32),
        jax.ShapeDtypeStruct((3, 256, 256), F32),
        jax.ShapeDtypeStruct((576, 768), BF16),
    )
    hbm = pl.BlockSpec(memory_space=pltpu.HBM)

    def stay(value):
        return pltpu.with_memory_space_constraint(value, pltpu.HBM)

    pg, qb = pl.pallas_call(
        tiles_kernel,
        out_shape=(wide, wide),
        in_specs=[smem] + [hbm] * 5,
        out_specs=(vmem, vmem),
        scratch_shapes=list(TILES_SCRATCH.values()),
        compiler_params=pltpu.CompilerParams(vmem_limit_bytes=TILES_LIMIT * 2**20),
        name="tiles",
    )(tile_counts, *[stay(v) for v in (tile_rows, tile_cols, pre_act, cotangent, tile_blocks)])
    found = pl.pallas_call(
        rest_kernel,
        out_shape=results,
        in_specs=[smem] * 2 + [vmem] * 3 + [hbm] * 3 + [vmem, hbm, vmem, vmem],
        out_specs=(vmem,) * 5,
        scratch_shapes=list(REST_SCRATCH.values()) + [kind for group in GROUPS for kind in group_scratch(group[2]).values()],
        compiler_params=pltpu.CompilerParams(collective_id=0, has_side_effects=True, vmem_limit_bytes=REST_LIMIT * 2**20),
        name="rest",
    )(send_counts, recv_counts, pg, qb, states, stay(features), stay(halo_states), stay(halo_cot), coupling.T, stay(send_rows), w_state, w_input)
    return pl.pallas_call(
        move_kernel,
        out_shape=results,
        in_specs=[vmem] * 5,
        out_specs=(far,) * 5,
        scratch_shapes=[pltpu.SemaphoreType.DMA((5,))],
        compiler_params=pltpu.CompilerParams(vmem_limit_bytes=2**20),
        name="move",
    )(*found)


TILES_LIMIT = 20
REST_LIMIT = 24


def solution(mesh):
    rows = P("dom", None)
    one = P("dom")
    return jax.shard_map(
        shards,
        mesh=mesh,
        in_specs=(rows,) * 7 + (P("dom", None, None), one, one, one, rows, one, one, P(), P()),
        out_specs=(rows, rows, P(), P(), rows),
        check_vma=False,
    )
```

profile of v0, /device:TPU:1, one launch (start us, length us, event | category | flops | bytes accessed | tf_op | source)
XLA Modules:
  0.0 54.4 jit_solution(17553578137803865039)
XLA Ops:
  1.3 0.0 copy-start
  1.3 0.0 copy-start.1
  1.3 0.0 copy-start.2
  1.3 0.0 copy-start.3
  1.3 0.0 copy-start.4
  1.3 0.0 copy-start.5
  1.3 8.2 %tiles.1 = (bf16[2048,768]{1,0:T(8,128)(2,1)S(1)}, bf16[2048,768]{1,0:T(8,128)(2,1)S(1)}) custom-call(s32[1]{0:T(128)S(6)} %copy.21.tile_counts, s32[64]{0:T(128)} %tile_rows.1, s32[64]{0:T(128)} %tile_cols.1, bf16[2048,768]{1,0:T(8,128)(2,1)} %pre_act.1, bf16[2048,256]{1,0:T(8,128)(2,1)} %cotangent.1, bf16[64,128,128]{2,1,0:T(8,128)(2,1)} %tile_blocks.1), custom_call_target="tpu_custom_call" | custom-call | tf_op jit(solution)/shard_map/tiles/pallas_call | solution.py:504
  9.5 0.0 copy-done
  9.5 0.0 copy-done.1
  9.5 0.0 copy-done.2
  9.5 0.0 copy-done.3
  9.5 0.0 copy-done.4
  9.6 0.0 copy-done.5
  9.6 42.0 %rest.1 = (bf16[2048,768]{1,0:T(8,128)(2,1)S(1)}, bf16[2048,256]{1,0:T(8,128)(2,1)S(1)}, f32[3,256,256]{2,1,0:T(8,128)S(1)}, f32[3,256,256]{2,1,0:T(8,128)S(1)}, bf16[576,768]{1,0:T(8,128)(2,1)S(1)}) custom-call(s32[9]{0:T(128)S(1)} %copy-done.4, s32[9]{0:T(128)S(1)} %copy-done.5, bf16[2048,768]{1,0:T(8,128)(2,1)S(1)} %get-tuple-element.12.refs_2_, ...), custom_call_target="tpu_custom_call" | custom-call | tf_op jit(solution)/shard_map/rest/pallas_call | solution.py:513
  51.6 2.8 %move.1 = (bf16[2048,768]{1,0:T(8,128)(2,1)}, bf16[2048,256]{1,0:T(8,128)(2,1)}, f32[3,256,256]{2,1,0:T(8,128)}, f32[3,256,256]{2,1,0:T(8,128)}, bf16[576,768]{1,0:T(8,128)(2,1)}) custom-call(bf16[2048,768]{1,0:T(8,128)(2,1)S(1)} %get-tuple-element.14.refs_0_, bf16[2048,256]{1,0:T(8,128)(2,1)S(1)} %get-tuple-element.15.refs_1_, ...), custom_call_target="tpu_custom_call" | custom-call | tf_op jit(solution)/shard_map/move/pallas_call | solution.py:522
Async XLA Ops:
  1.3 8.2 %copy-start = (bf16[2048,768]{1,0:T(8,128)(2,1)S(1)}, bf16[2048,768]{1,0:T(8,128)(2,1)}, u32[]{:S(2)}) copy-start(bf16[2048,768]{1,0:T(8,128)(2,1)} %refs_4_.1) | copy-start | bytes 9437188
  1.3 8.2 %copy-start.1 = (bf16[2048,576]{0,1:T(8,128)(2,1)S(1)}, bf16[2048,576]{0,1:T(8,128)(2,1)}, u32[]{:S(2)}) copy-start(bf16[2048,576]{0,1:T(8,128)(2,1)} %param.22) | copy-start | bytes 7077892
  1.3 8.2 %copy-start.2 = (bf16[3,256,256]{2,1,0:T(8,128)(2,1)S(1)}, bf16[3,256,256]{2,1,0:T(8,128)(2,1)}, u32[]{:S(2)}) copy-start(bf16[3,256,256]{2,1,0:T(8,128)(2,1)} %refs_10_.1) | copy-start | bytes 1179652
  1.3 8.2 %copy-start.3 = (bf16[3,256,256]{2,1,0:T(8,128)(2,1)S(1)}, bf16[3,256,256]{2,1,0:T(8,128)(2,1)}, u32[]{:S(2)}) copy-start(bf16[3,256,256]{2,1,0:T(8,128)(2,1)} %refs_11_.1) | copy-start | bytes 1179652
  1.3 8.2 %copy-start.4 = (s32[9]{0:T(128)S(1)}, s32[9]{0:T(128)}, u32[]{:S(2)}) copy-start(s32[9]{0:T(128)} %refs_0_.1) | copy-start | bytes 112
  1.3 8.2 %copy-start.5 = (s32[9]{0:T(128)S(1)}, s32[9]{0:T(128)}, u32[]{:S(2)}) copy-start(s32[9]{0:T(128)} %refs_1_.1) | copy-start | bytes 112
where the time goes:
time: 54.5 us; the launch traced here: 54.4 us
  Pallas kernels  53 us (97%)
  between operations  1.39 us (3%)
    pallas_call x1, Pallas kernels, shards(): pl.pallas_call(rest_kernel, out_shape=results, in_specs=[smem] * 2 + [vme...  42 us
    pallas_call x1, Pallas kernels, shards(): pl.pallas_call(tiles_kernel, out_shape=(wide, wide), in_specs=[smem] + [h...  8.15 us
    pallas_call x1, Pallas kernels, shards(): pl.pallas_call(move_kernel, out_shape=results, in_specs=[vmem] * 5, out_s...  2.81 us

commit v1 on v0

--- a/solution.py
+++ b/solution.py
@@ -73,11 +73,10 @@
     def total(mask, value):
         return jnp.sum(jnp.where(mask, value, 0), axis=0, keepdims=True)
 
-    meta = (total(first, tile - 64) + 64, total(second, tile - 64) + 64, total(first, row), total(second, row), total(first & (place > 0), 1), upto, inside)
+    meta = (total(first, tile - 64) + 64, total(second, tile - 64) + 64, total(first, row), total(second, row), total(first & (place > 0), 1), upto, jnp.minimum(inside, 1))
     for i, value in enumerate(meta):
-        r.v_meta[i : i + 1, :] = value
-    r.v_meta[7:8, :] = jnp.zeros((1, 128), jnp.int32)
-    pltpu.make_async_copy(r.v_meta, r.meta, r.meta_sem).start()
+        r.meta[i : i + 1, :] = value
+    r.meta[7:8, :] = jnp.zeros((1, 128), jnp.int32)
 
 
 def make_pre_grad(r):
@@ -138,29 +137,27 @@
 
 
 def flip_tiles(r):
-    r.v_tile_blocks[64] = jnp.zeros((128, 128), BF16)
+    r.tiles[64] = jnp.zeros((128, 128), BF16)
     r.load_tile_blocks.wait()
 
     @pl.loop(0, 64, unroll=16)
     def _(t):
-        r.v_tile_blocks[t] = r.v_tile_blocks[t].T
+        r.tiles[t] = r.tiles[t].T
 
 
 def make_q(r, k):
     cols = slice(256 * k, 256 * k + 256)
-    meta, tiles = r.meta, r.v_tile_blocks
+    meta, tiles = r.meta, r.tiles
 
     @pl.loop(0, 40, unroll=20)
     def _(t):
-        up = pl.ds(pl.multiple_of(meta[2, t] * 128, 128), 128)
-        low = pl.ds(pl.multiple_of(meta[3, t] * 128, 128), 128)
         left = jnp.concatenate([tiles[meta[0, t]], tiles[meta[1, t]]], axis=1)
-        right = jnp.concatenate([r.pg[up, cols], r.pg[low, cols]], axis=0)
-        r.stage[t + 1] = dot(left, right) + jnp.where(meta[4, t] > 0, r.stage[t], 0.0)
+        right = jnp.concatenate([r.blocked[meta[2, t], :, cols], r.blocked[meta[3, t], :, cols]], axis=0)
+        r.stage[t + 1] = dot(left, right) + r.stage[t] * meta[4, t].astype(F32)
 
     @pl.loop(0, 16, unroll=8)
     def _(c):
-        value = jnp.where(meta[6, c] > 0, r.stage[meta[5, c]], 0.0)
+        value = r.stage[meta[5, c]] * meta[6, c].astype(F32)
         r.qb[pl.ds(pl.multiple_of(c * 128, 128), 128), cols] = value.astype(BF16)
 
 
@@ -342,21 +339,16 @@
     )
 
 
-TILES_SCRATCH = dict(
+FIRST_SCRATCH = dict(
     ct=pltpu.VMEM((2048, 256), BF16),
-    v_tile_blocks=pltpu.VMEM((65, 128, 128), BF16),
-    stage=pltpu.VMEM((41, 128, 256), F32),
-    meta=pltpu.SMEM((8, 128), jnp.int32),
-    v_meta=pltpu.VMEM((8, 128), jnp.int32),
     s_tile_rows=pltpu.SMEM((64,), jnp.int32),
     s_tile_cols=pltpu.SMEM((64,), jnp.int32),
     in_sem=DMA((11,)),
-    meta_sem=DMA(()),
 )
 
 
-def tiles_kernel(tile_counts, tile_rows, tile_cols, pre_act, cotangent, tile_blocks, pg, qb, *scratch):
-    r = SimpleNamespace(**dict(zip(TILES_SCRATCH, scratch, strict=True)), tile_counts=tile_counts, pg=pg, qb=qb)
+def first_kernel(tile_counts, tile_rows, tile_cols, pre_act, cotangent, tile_blocks, pg, tiles, meta, *scratch):
+    r = SimpleNamespace(**dict(zip(FIRST_SCRATCH, scratch, strict=True)), tile_counts=tile_counts, pg=pg, tiles=tiles, meta=meta)
 
     def load(i, src, dst):
         copy = pltpu.make_async_copy(src, dst, r.in_sem.at[i])
@@ -370,17 +362,15 @@
     for i, rows in enumerate(parts):
         r.load_cots.append(load(2 + i, cotangent.at[rows], r.ct.at[rows]))
         r.load_acts.append(load(6 + i, pre_act.at[rows], pg.at[rows]))
-    r.load_tile_blocks = load(10, tile_blocks, r.v_tile_blocks.at[pl.ds(0, 64)])
+    r.load_tile_blocks = load(10, tile_blocks, tiles.at[pl.ds(0, 64)])
     order_tiles(r)
-    r.stage[0] = jnp.zeros((128, 256), F32)
     make_pre_grad(r)
     flip_tiles(r)
-    pltpu.make_async_copy(r.v_meta, r.meta, r.meta_sem).wait()
-    for k in range(3):
-        make_q(r, k)
 
 
 REST_SCRATCH = dict(
+    stage=pltpu.VMEM((41, 128, 256), F32),
+    qb=pltpu.VMEM((2048, 768), BF16),
     v_send_rows=pltpu.VMEM((9, 64), jnp.int32),
     v_features=pltpu.VMEM((2048, 256), BF16),
     v_halo_states=pltpu.VMEM((576, 768), BF16),
@@ -395,11 +385,11 @@
 )
 
 
-def rest_refs(send_counts, recv_counts, pg, qb, states, features, halo_states, halo_cot, coupling, send_rows, w_state, w_input, state_grad, feature_grad, weight_grad, input_grad, sent_cot, *scratch):
+def rest_refs(send_counts, recv_counts, meta, pg, blocked, tiles, states, features, halo_states, halo_cot, coupling, send_rows, w_state, w_input, state_grad, feature_grad, weight_grad, input_grad, sent_cot, *scratch):
     scratch = list(scratch)
     own = dict(zip(REST_SCRATCH, scratch))
     del scratch[: len(own)]
-    r = SimpleNamespace(**own, send_counts=send_counts, recv_counts=recv_counts, pg=pg, qb=qb, states=states, coupling=coupling, w_state=w_state, w_input=w_input)
+    r = SimpleNamespace(**own, send_counts=send_counts, recv_counts=recv_counts, meta=meta, pg=pg, blocked=blocked, tiles=tiles, states=states, coupling=coupling, w_state=w_state, w_input=w_input)
     r.state_grad, r.feature_grad, r.weight_grad, r.input_grad, r.sent_cot = state_grad, feature_grad, weight_grad, input_grad, sent_cot
     r.groups = []
     for p, k, count in GROUPS:
@@ -429,14 +419,18 @@
         for j in slots:
             halo_copy(r, at, j).start()
 
+    r.stage[0] = jnp.zeros((128, 256), F32)
+    make_q(r, 0)
     r.load_halo_states.wait()
     mask_halo(r, r.v_halo_states)
     make_w(r, 0)
     await_greetings()
     reduce_core(r, at, w0)
+    make_q(r, 1)
     make_w(r, 1)
     reduce_core(r, at, w1)
     reduce_plane(r, at, w0)
+    make_q(r, 2)
     make_w(r, 2)
     reduce_core(r, at, w2)
     reduce_plane(r, at, w1)
@@ -449,26 +443,26 @@
     reduce_plane(r, at, v)
     make_outgoing(r, 1)
     make_outgoing(r, 2)
-    halo(2, 6)
     reduce_line(r, at, w1)
+    halo(3, 7)
     make_e(r)
+    make_feature_grad(r)
     reduce_line(r, at, w2)
     gather_plane(r, at, w0)
-    halo(3, 7)
-    make_feature_grad(r)
+    halo(2, 6)
+    make_state_grad(r, 0)
+    reduce_line(r, at, v)
     gather_plane(r, at, w1)
-    reduce_line(r, at, v)
-    make_state_grad(r, 0)
     gather_plane(r, at, w2)
     halo(1, 5)
-    gather_core(r, at, w0)
     make_state_grad(r, 1)
     gather_plane(r, at, v)
     halo(0, 4, 8)
+    gather_core(r, at, w0)
+    gather_core(r, at, w1)
     gather_end(r, at, w0)
-    gather_core(r, at, w1)
+    gather_end(r, at, w1)
     gather_core(r, at, w2)
-    gather_end(r, at, w1)
     gather_end(r, at, w2)
     gather_core(r, at, v)
     gather_end(r, at, v)
@@ -501,24 +495,24 @@
     def stay(value):
         return pltpu.with_memory_space_constraint(value, pltpu.HBM)
 
-    pg, qb = pl.pallas_call(
-        tiles_kernel,
-        out_shape=(wide, wide),
+    pg, tiles, meta = pl.pallas_call(
+        first_kernel,
+        out_shape=(wide, jax.ShapeDtypeStruct((65, 128, 128), BF16), jax.ShapeDtypeStruct((8, 128), jnp.int32)),
         in_specs=[smem] + [hbm] * 5,
-        out_specs=(vmem, vmem),
-        scratch_shapes=list(TILES_SCRATCH.values()),
-        compiler_params=pltpu.CompilerParams(vmem_limit_bytes=TILES_LIMIT * 2**20),
-        name="tiles",
+        out_specs=(vmem,) * 3,
+        scratch_shapes=list(FIRST_SCRATCH.values()),
+        compiler_params=pltpu.CompilerParams(vmem_limit_bytes=FIRST_LIMIT * 2**20),
+        name="first",
     )(tile_counts, *[stay(v) for v in (tile_rows, tile_cols, pre_act, cotangent, tile_blocks)])
     found = pl.pallas_call(
         rest_kernel,
         out_shape=results,
-        in_specs=[smem] * 2 + [vmem] * 3 + [hbm] * 3 + [vmem, hbm, vmem, vmem],
+        in_specs=[smem] * 3 + [vmem] * 4 + [hbm] * 3 + [vmem, hbm, vmem, vmem],
         out_specs=(vmem,) * 5,
         scratch_shapes=list(REST_SCRATCH.values()) + [kind for group in GROUPS for kind in group_scratch(group[2]).values()],
         compiler_params=pltpu.CompilerParams(collective_id=0, has_side_effects=True, vmem_limit_bytes=REST_LIMIT * 2**20),
         name="rest",
-    )(send_counts, recv_counts, pg, qb, states, stay(features), stay(halo_states), stay(halo_cot), coupling.T, stay(send_rows), w_state, w_input)
+    )(send_counts, recv_counts, meta, pg, pg.reshape(16, 128, 768), tiles, states, stay(features), stay(halo_states), stay(halo_cot), coupling.T, stay(send_rows), w_state, w_input)
     return pl.pallas_call(
         move_kernel,
         out_shape=results,
@@ -530,8 +524,8 @@
     )(*found)
 
 
-TILES_LIMIT = 20
-REST_LIMIT = 24
+FIRST_LIMIT = 14
+REST_LIMIT = 32
 
 
 def solution(mesh):

time: 54.5 us -> 51.3 us (0.941)
  Pallas kernels: 53 us -> 49.1 us
  local copies, waits for them, and re-layouts: 0.03 us -> 0.7 us
    pallas_call x2, Pallas kernels: 50.2 us -> 46.3 us  [the longest x1 42.5 us: shards(): pl.pallas_call(rest_kernel, out_shape=results, in_specs=[smem] * 3 + [vme...]
    unnamed x12, local copies, waits for them, and re-layouts: 0.03 us -> 0.7 us
where the time goes in v1:
time: 51.3 us; the launch traced here: 51.2 us
  Pallas kernels  49.1 us (96%)
  between operations  1.36 us (3%)
  local copies, waits for them, and re-layouts  0.7 us (1%)
    pallas_call x1, Pallas kernels, shards(): pl.pallas_call(rest_kernel, out_shape=results, in_specs=[smem] * 3 + [vme...  42.5 us
    pallas_call x1, Pallas kernels, shards(): pl.pallas_call(first_kernel, out_shape=(wide, jax.ShapeDtypeStruct((65, 1...  3.86 us
    pallas_call x1, Pallas kernels, shards(): pl.pallas_call(move_kernel, out_shape=results, in_specs=[vmem] * 5, out_s...  2.81 us

profile of v1, /device:TPU:1, one launch (start us, length us, event | category | flops | bytes accessed | tf_op | source)
XLA Modules:
  0.0 51.2 jit_solution(5950371420831822825)
XLA Ops:
  1.3 0.0 copy-start
  1.3 0.0 copy-start.1
  1.3 0.0 copy-start.2
  1.3 0.0 copy-start.3
  1.3 0.0 copy-start.4
  1.3 0.0 copy-start.5
  1.3 3.9 %first.1 = (bf16[2048,768]{1,0:T(8,128)(2,1)S(1)}, bf16[65,128,128]{2,1,0:T(8,128)(2,1)S(1)}, s32[8,128]{1,0:T(8,128)S(1)}) custom-call(s32[1]{0:T(128)S(6)} %copy.21.tile_counts, s32[64]{0:T(128)} %tile_rows.1, s32[64]{0:T(128)} %tile_cols.1, bf16[2048,768]{1,0:T(8,128)(2,1)} %pre_act.1, bf16[2048,256]{1,0:T(8,128)(2,1)} %cotangent.1, ...), custom_call_target="tpu_custom_call" | custom-call | tf_op jit(solution)/shard_map/first/pallas_call | solution.py:498
  5.2 0.0 copy-done
  5.2 0.5 %copy-done.1 = bf16[2048,576]{0,1:T(8,128)(2,1)S(1)} copy-done((bf16[2048,576]{0,1:T(8,128)(2,1)S(1)}, bf16[2048,576]{0,1:T(8,128)(2,1)}, u32[]{:S(2)}) %copy-start.1) | copy-done | bytes 2359320
  5.8 0.0 copy-done.2
  5.8 0.1 copy-done.3
  5.9 0.0 copy-done.4
  5.9 0.0 copy-done.5
  5.9 42.5 %rest.1 = (bf16[2048,768]{1,0:T(8,128)(2,1)S(1)}, bf16[2048,256]{1,0:T(8,128)(2,1)S(1)}, f32[3,256,256]{2,1,0:T(8,128)S(1)}, f32[3,256,256]{2,1,0:T(8,128)S(1)}, bf16[576,768]{1,0:T(8,128)(2,1)S(1)}) custom-call(s32[9]{0:T(128)S(1)} %copy-done.4, s32[9]{0:T(128)S(1)} %copy-done.5, s32[8,128]{1,0:T(8,128)S(1)} %get-tuple-element.13.refs_2_, ...), custom_call_target="tpu_custom_call" | custom-call | tf_op jit(solution)/shard_map/rest/pallas_call | solution.py:507
  48.4 2.8 %move.1 = (bf16[2048,768]{1,0:T(8,128)(2,1)}, bf16[2048,256]{1,0:T(8,128)(2,1)}, f32[3,256,256]{2,1,0:T(8,128)}, f32[3,256,256]{2,1,0:T(8,128)}, bf16[576,768]{1,0:T(8,128)(2,1)}) custom-call(bf16[2048,768]{1,0:T(8,128)(2,1)S(1)} %get-tuple-element.16.refs_0_, bf16[2048,256]{1,0:T(8,128)(2,1)S(1)} %get-tuple-element.17.refs_1_, ...), custom_call_target="tpu_custom_call" | custom-call | tf_op jit(solution)/shard_map/move/pallas_call | solution.py:516
Async XLA Ops:
  1.3 3.9 %copy-start = (bf16[2048,768]{1,0:T(8,128)(2,1)S(1)}, bf16[2048,768]{1,0:T(8,128)(2,1)}, u32[]{:S(2)}) copy-start(bf16[2048,768]{1,0:T(8,128)(2,1)} %refs_6_.1) | copy-start | bytes 9437188
  1.3 4.5 %copy-start.1 = (bf16[2048,576]{0,1:T(8,128)(2,1)S(1)}, bf16[2048,576]{0,1:T(8,128)(2,1)}, u32[]{:S(2)}) copy-start(bf16[2048,576]{0,1:T(8,128)(2,1)} %param.22) | copy-start | bytes 7077892
  1.3 4.5 %copy-start.2 = (bf16[3,256,256]{2,1,0:T(8,128)(2,1)S(1)}, bf16[3,256,256]{2,1,0:T(8,128)(2,1)}, u32[]{:S(2)}) copy-start(bf16[3,256,256]{2,1,0:T(8,128)(2,1)} %refs_12_.1) | copy-start | bytes 1179652
  1.3 4.6 %copy-start.3 = (bf16[3,256,256]{2,1,0:T(8,128)(2,1)S(1)}, bf16[3,256,256]{2,1,0:T(8,128)(2,1)}, u32[]{:S(2)}) copy-start(bf16[3,256,256]{2,1,0:T(8,128)(2,1)} %refs_13_.1) | copy-start | bytes 1179652
  1.3 4.6 %copy-start.4 = (s32[9]{0:T(128)S(1)}, s32[9]{0:T(128)}, u32[]{:S(2)}) copy-start(s32[9]{0:T(128)} %refs_0_.1) | copy-start | bytes 112
  1.3 4.6 %copy-start.5 = (s32[9]{0:T(128)S(1)}, s32[9]{0:T(128)}, u32[]{:S(2)}) copy-start(s32[9]{0:T(128)} %refs_1_.1) | copy-start | bytes 112

commit v2 on v1

--- a/solution.py
+++ b/solution.py
@@ -232,6 +232,17 @@
     return remote(r.outgoing.at[rows], r.sent_cot.at[rows], r.halo_send.at[j], r.halo_recv.at[j], at.halo[j])
 
 
+def halo_start(r, at, j):
+    if j == SLOTS - 1:
+        halo_copy(r, at, j).start()
+        return
+    flip = 1 - 2 * at.core
+    slot = j + at.core * (4 if j < 4 else -4)
+    rows = pl.ds(pl.multiple_of(slot * CAP, CAP), CAP)
+    device = lax.rem(at.me + 128 + flip * OFFSETS[j], 128)
+    remote(r.outgoing.at[rows], r.sent_cot.at[rows], r.halo_send.at[slot], r.halo_recv.at[slot], device).start()
+
+
 def core_copy(at, g):
     return remote(g.half, g.core, g.a_send, g.a_recv, at.sibling)
 
@@ -417,7 +428,7 @@
 
     def halo(*slots):
         for j in slots:
-            halo_copy(r, at, j).start()
+            halo_start(r, at, j)
 
     r.stage[0] = jnp.zeros((128, 256), F32)
     make_q(r, 0)
@@ -426,46 +437,45 @@
     make_w(r, 0)
     await_greetings()
     reduce_core(r, at, w0)
+    make_v(r)
+    reduce_core(r, at, v)
+    reduce_plane(r, at, w0)
+    make_one_hot(r)
+    make_outgoing(r, 0)
+    reduce_plane(r, at, v)
+    make_outgoing(r, 1)
+    make_outgoing(r, 2)
+    halo(3, 7, 8)
     make_q(r, 1)
     make_w(r, 1)
     reduce_core(r, at, w1)
-    reduce_plane(r, at, w0)
+    reduce_line(r, at, w0)
+    reduce_line(r, at, v)
+    halo(2, 6)
     make_q(r, 2)
+    reduce_plane(r, at, w1)
     make_w(r, 2)
     reduce_core(r, at, w2)
-    reduce_plane(r, at, w1)
-    make_v(r)
-    reduce_core(r, at, v)
+    gather_plane(r, at, w0)
+    gather_plane(r, at, v)
+    make_e(r)
     reduce_plane(r, at, w2)
-    make_one_hot(r)
-    make_outgoing(r, 0)
-    reduce_line(r, at, w0)
-    reduce_plane(r, at, v)
-    make_outgoing(r, 1)
-    make_outgoing(r, 2)
+    halo(1, 5, 0, 4)
+    make_feature_grad(r)
     reduce_line(r, at, w1)
-    halo(3, 7)
-    make_e(r)
-    make_feature_grad(r)
+    make_state_grad(r, 0)
     reduce_line(r, at, w2)
-    gather_plane(r, at, w0)
-    halo(2, 6)
-    make_state_grad(r, 0)
-    reduce_line(r, at, v)
+    gather_core(r, at, w0)
+    gather_core(r, at, v)
     gather_plane(r, at, w1)
+    make_state_grad(r, 1)
     gather_plane(r, at, w2)
-    halo(1, 5)
-    make_state_grad(r, 1)
-    gather_plane(r, at, v)
-    halo(0, 4, 8)
-    gather_core(r, at, w0)
+    gather_end(r, at, w0)
+    gather_end(r, at, v)
     gather_core(r, at, w1)
-    gather_end(r, at, w0)
     gather_end(r, at, w1)
     gather_core(r, at, w2)
     gather_end(r, at, w2)
-    gather_core(r, at, v)
-    gather_end(r, at, v)
     drain(r, at)
 
 

time: 51.3 us -> 50.5 us (0.984)
  Pallas kernels: 49.1 us -> 48.3 us
    pallas_call x1, Pallas kernels: 42.5 us -> 41.7 us  [shards(): pl.pallas_call(rest_kernel, out_shape=results, in_specs=[smem] * 3 + [vme...]
where the time goes in v2:
time: 50.5 us; the launch traced here: 50.4 us
  Pallas kernels  48.3 us (96%)
  between operations  1.36 us (3%)
  local copies, waits for them, and re-layouts  0.7 us (1%)
    pallas_call x1, Pallas kernels, shards(): pl.pallas_call(rest_kernel, out_shape=results, in_specs=[smem] * 3 + [vme...  41.7 us
    pallas_call x1, Pallas kernels, shards(): pl.pallas_call(first_kernel, out_shape=(wide, jax.ShapeDtypeStruct((65, 1...  3.86 us
    pallas_call x1, Pallas kernels, shards(): pl.pallas_call(move_kernel, out_shape=results, in_specs=[vmem] * 5, out_s...  2.81 us

profile of v2, /device:TPU:1, one launch (start us, length us, event | category | flops | bytes accessed | tf_op | source)
XLA Modules:
  0.0 50.4 jit_solution(14936507710150535945)
XLA Ops:
  1.3 0.0 copy-start
  1.3 0.0 copy-start.1
  1.3 0.0 copy-start.2
  1.3 0.0 copy-start.3
  1.3 0.0 copy-start.4
  1.3 0.0 copy-start.5
  1.3 3.9 %first.1 = (bf16[2048,768]{1,0:T(8,128)(2,1)S(1)}, bf16[65,128,128]{2,1,0:T(8,128)(2,1)S(1)}, s32[8,128]{1,0:T(8,128)S(1)}) custom-call(s32[1]{0:T(128)S(6)} %copy.21.tile_counts, s32[64]{0:T(128)} %tile_rows.1, s32[64]{0:T(128)} %tile_cols.1, bf16[2048,768]{1,0:T(8,128)(2,1)} %pre_act.1, bf16[2048,256]{1,0:T(8,128)(2,1)} %cotangent.1, ...), custom_call_target="tpu_custom_call" | custom-call | tf_op jit(solution)/shard_map/first/pallas_call | solution.py:508
  5.2 0.0 copy-done
  5.2 0.5 %copy-done.1 = bf16[2048,576]{0,1:T(8,128)(2,1)S(1)} copy-done((bf16[2048,576]{0,1:T(8,128)(2,1)S(1)}, bf16[2048,576]{0,1:T(8,128)(2,1)}, u32[]{:S(2)}) %copy-start.1) | copy-done | bytes 2359320
  5.8 0.0 copy-done.2
  5.8 0.1 copy-done.3
  5.9 0.0 copy-done.4
  5.9 0.0 copy-done.5
  5.9 41.7 %rest.1 = (bf16[2048,768]{1,0:T(8,128)(2,1)S(1)}, bf16[2048,256]{1,0:T(8,128)(2,1)S(1)}, f32[3,256,256]{2,1,0:T(8,128)S(1)}, f32[3,256,256]{2,1,0:T(8,128)S(1)}, bf16[576,768]{1,0:T(8,128)(2,1)S(1)}) custom-call(s32[9]{0:T(128)S(1)} %copy-done.4, s32[9]{0:T(128)S(1)} %copy-done.5, s32[8,128]{1,0:T(8,128)S(1)} %get-tuple-element.13.refs_2_, ...), custom_call_target="tpu_custom_call" | custom-call | tf_op jit(solution)/shard_map/rest/pallas_call | solution.py:517
  47.6 2.8 %move.1 = (bf16[2048,768]{1,0:T(8,128)(2,1)}, bf16[2048,256]{1,0:T(8,128)(2,1)}, f32[3,256,256]{2,1,0:T(8,128)}, f32[3,256,256]{2,1,0:T(8,128)}, bf16[576,768]{1,0:T(8,128)(2,1)}) custom-call(bf16[2048,768]{1,0:T(8,128)(2,1)S(1)} %get-tuple-element.16.refs_0_, bf16[2048,256]{1,0:T(8,128)(2,1)S(1)} %get-tuple-element.17.refs_1_, ...), custom_call_target="tpu_custom_call" | custom-call | tf_op jit(solution)/shard_map/move/pallas_call | solution.py:526
Async XLA Ops:
  1.3 3.9 %copy-start = (bf16[2048,768]{1,0:T(8,128)(2,1)S(1)}, bf16[2048,768]{1,0:T(8,128)(2,1)}, u32[]{:S(2)}) copy-start(bf16[2048,768]{1,0:T(8,128)(2,1)} %refs_6_.1) | copy-start | bytes 9437188
  1.3 4.5 %copy-start.1 = (bf16[2048,576]{0,1:T(8,128)(2,1)S(1)}, bf16[2048,576]{0,1:T(8,128)(2,1)}, u32[]{:S(2)}) copy-start(bf16[2048,576]{0,1:T(8,128)(2,1)} %param.22) | copy-start | bytes 7077892
  1.3 4.5 %copy-start.2 = (bf16[3,256,256]{2,1,0:T(8,128)(2,1)S(1)}, bf16[3,256,256]{2,1,0:T(8,128)(2,1)}, u32[]{:S(2)}) copy-start(bf16[3,256,256]{2,1,0:T(8,128)(2,1)} %refs_12_.1) | copy-start | bytes 1179652
  1.3 4.6 %copy-start.3 = (bf16[3,256,256]{2,1,0:T(8,128)(2,1)S(1)}, bf16[3,256,256]{2,1,0:T(8,128)(2,1)}, u32[]{:S(2)}) copy-start(bf16[3,256,256]{2,1,0:T(8,128)(2,1)} %refs_13_.1) | copy-start | bytes 1179652
  1.3 4.6 %copy-start.4 = (s32[9]{0:T(128)S(1)}, s32[9]{0:T(128)}, u32[]{:S(2)}) copy-start(s32[9]{0:T(128)} %refs_0_.1) | copy-start | bytes 112
  1.3 4.6 %copy-start.5 = (s32[9]{0:T(128)S(1)}, s32[9]{0:T(128)}, u32[]{:S(2)}) copy-start(s32[9]{0:T(128)} %refs_1_.1) | copy-start | bytes 112
